TPU v7x, 32 devices: a whole 2x2x4 slice. The times are simulated.
32 devices in a mesh: lag: 4 (over z), probe: 4 (over y, x), sketch: 2 (over core).
Axes of the slice: x: 2, y: 2, z: 4, core: 2. Of those that a mesh axis runs over, the one named last changes fastest.
Arguments:
- markov: bfloat16 [16, 32, 8192], P('lag', None, ('probe', 'sketch')), may hold values from -36 to 36
- test_matrix: bfloat16 [4, 32, 256], P('lag', None, 'sketch'), may hold values from -0.5 to 0.5
Outputs:
- sketch_out: bfloat16 [16, 8192, 256], P('lag', 'probe', 'sketch')
All inputs are finite; a program needn't handle non-finite values.
Results may differ from a plain program's by a relative error of at most 0.0004.
Values may be sent and summed in bfloat16 or wider, within the bound.
A program may use at most 64 MiB of HBM per device.

v0:
```python
import functools

import jax
import jax.numpy as jnp
from jax import lax
from jax.experimental import pallas as pl
from jax.experimental.pallas import tpu as pltpu
from jax.sharding import PartitionSpec as P

MESH = pl.DeviceIdType.MESH
UNROLL = 32


def loop(count, body):
    if count <= UNROLL:
        for index in range(count):
            body(index)
    else:
        def step(index, carry):
            body(index)
            return carry
        lax.fori_loop(0, count, step, 0)


def plan(step_count, lag_total):
    steps = step_count + lag_total - 1
    blocks = (steps - 1) // step_count
    pieces = []
    for ahead in range(1, blocks + 1):
        used = min(step_count, steps - ahead * step_count)
        if blocks == 1:
            pieces += [(ahead, at, 1) for at in range(used)]
        else:
            pieces.append((ahead, 0, used))
    return steps, pieces


def gather_kernel(
    sizes, markov, matrix, raw, factor,
    window, held, weights, sums,
    own_sem, matrix_own_sem, matrix_send, matrix_recv,
    pair_send, pair_recv, lag_send, lag_recv, next_send, next_recv, sum_send, sum_recv,
):
    n_lag, n_probe, n_sketch = sizes
    step_count, input_count, half = markov.shape
    matrix_rows = matrix.shape[0]
    columns = matrix.shape[2]
    lag_total = matrix_rows * n_lag
    steps, pieces = plan(step_count, lag_total)
    lag = lax.axis_index("lag")
    probe = lax.axis_index("probe")
    sketch = lax.axis_index("sketch")
    flat = lag * n_probe + probe
    peers = n_lag * n_probe - 1

    def peer(index):
        other = lax.rem(flat + 1 + index, peers + 1)
        return {
            "lag": lax.div(other, n_probe),
            "probe": lax.rem(other, n_probe),
            "sketch": sketch,
        }

    def partner(index):
        return {"lag": lag, "probe": probe, "sketch": lax.rem(sketch + 1 + index, n_sketch)}

    def lag_peer(index):
        return {"lag": lax.rem(lag + 1 + index, n_lag), "probe": probe, "sketch": sketch}

    barrier = pltpu.get_barrier_semaphore()

    def greet(index):
        pl.semaphore_signal(barrier, inc=1, device_id=peer(index), device_id_type=MESH)

    for index in range(n_sketch - 1):
        pl.semaphore_signal(barrier, inc=1, device_id=partner(index), device_id_type=MESH)
    loop(peers, greet)

    own = pltpu.make_async_copy(markov, window.at[sketch, pl.ds(0, step_count)], own_sem)
    own.start()
    matrix_own = pltpu.make_async_copy(
        matrix, held.at[pl.ds(lag * matrix_rows, matrix_rows)], matrix_own_sem
    )
    matrix_own.start()
    weights[...] = jnp.zeros_like(weights)
    for ahead, at, count in pieces:
        @pl.when(lag + ahead >= n_lag)
        def _():
            place = pl.ds(ahead * step_count + at, count)
            window[:, place] = jnp.zeros((n_sketch, count, input_count, half), window.dtype)

    matrix_own.wait()
    pl.semaphore_wait(barrier, peers + n_sketch - 1)

    def lag_copy(number):
        ahead, at, count = pieces[number]
        return pltpu.make_async_remote_copy(
            src_ref=markov.at[pl.ds(at, count)],
            dst_ref=window.at[sketch, pl.ds(ahead * step_count + at, count)],
            send_sem=lag_send.at[number],
            recv_sem=lag_recv.at[number],
            device_id={"lag": lax.max(lag - ahead, 0), "probe": probe, "sketch": sketch},
            device_id_type=MESH,
        )

    def pair_copy(index):
        return pltpu.make_async_remote_copy(
            src_ref=markov,
            dst_ref=window.at[sketch, pl.ds(0, step_count)],
            send_sem=pair_send.at[index],
            recv_sem=pair_recv.at[index],
            device_id=partner(index),
            device_id_type=MESH,
        )

    def next_copy(number, index):
        ahead, at, count = pieces[number]
        place = window.at[sketch, pl.ds(ahead * step_count + at, count)]
        return pltpu.make_async_remote_copy(
            src_ref=place,
            dst_ref=place,
            send_sem=next_send.at[number, index],
            recv_sem=next_recv.at[number, index],
            device_id=partner(index),
            device_id_type=MESH,
        )

    def matrix_copy(index):
        return pltpu.make_async_remote_copy(
            src_ref=held.at[pl.ds(lag * matrix_rows, matrix_rows)],
            dst_ref=held.at[pl.ds(lag * matrix_rows, matrix_rows)],
            send_sem=matrix_send,
            recv_sem=matrix_recv,
            device_id=lag_peer(index),
            device_id_type=MESH,
        )

    loop(n_lag - 1, lambda index: matrix_copy(index).start())
    for number in range(0, 1):
        @pl.when(lag >= pieces[number][0])
        def _():
            lag_copy(number).start()
    for index in range(n_sketch - 1):
        pair_copy(index).start()
    for number in range(1, len(pieces)):
        @pl.when(lag >= pieces[number][0])
        def _():
            lag_copy(number).start()

    if n_lag > 1:
        arrived = held.at[pl.ds(0, (n_lag - 1) * matrix_rows)]
        pltpu.make_async_copy(arrived, arrived, matrix_recv).wait()
        pltpu.make_async_copy(arrived, arrived, matrix_send).wait()
    for row in range(step_count):
        weights[pl.ds(row * input_count, lag_total * input_count), row * columns:(row + 1) * columns] = (
            held[...].reshape(lag_total * input_count, columns)
        )

    def forward(number):
        @pl.when(lag + pieces[number][0] < n_lag)
        def _():
            lag_copy(number).wait_recv()
            for index in range(n_sketch - 1):
                next_copy(number, index).start()

    def landed(number):
        @pl.when(lag + pieces[number][0] < n_lag)
        def _():
            for index in range(n_sketch - 1):
                next_copy(number, index).wait()

    tile = min(256, half)
    group = 2 if step_count % 2 == 0 else 1

    def compute(first, total):
        depth = (lag_total + group - 1) * input_count
        weight = weights[pl.ds(first * input_count, depth), first * columns:(first + group) * columns]
        for side in range(n_sketch):
            def body(at, total):
                start = pl.multiple_of(at * tile, tile)
                block = window[side, pl.ds(first, lag_total + group - 1), :, pl.ds(start, tile)]
                product = lax.dot_general(
                    block.reshape(depth, tile), weight, (((0,), (0,)), ((), ())),
                    preferred_element_type=jnp.float32,
                )
                for row in range(group):
                    part = product[:, row * columns:(row + 1) * columns]
                    raw[first + row, pl.ds(side * half + start, tile), :] = part
                    total = total + jnp.sum((part * part).reshape(tile // 8, 8, columns), axis=0)
                return total
            total = lax.fori_loop(0, half // tile, body, total, unroll=depth <= 512)
        return total

    own.wait()
    total = jnp.zeros((8, columns), jnp.float32)
    done = 0
    paired = False
    for first in range(0, step_count, group):
        need = first + group - 1 + lag_total
        ready = done
        while ready < len(pieces) and pieces[ready][0] * step_count + pieces[ready][1] < need:
            forward(ready)
            ready += 1
        if not paired:
            for index in range(n_sketch - 1):
                pair_copy(index).wait()
            paired = True
        for number in range(done, ready):
            landed(number)
        done = ready
        total = compute(first, total)

    sums[pl.ds(flat, 1), :] = jnp.sum(total, axis=0, keepdims=True)

    def sum_copy(index):
        place = sums.at[pl.ds(flat, 1)]
        return pltpu.make_async_remote_copy(
            src_ref=place,
            dst_ref=place,
            send_sem=sum_send,
            recv_sem=sum_recv,
            device_id=peer(index),
            device_id_type=MESH,
        )

    loop(peers, lambda index: sum_copy(index).start())
    for number in range(len(pieces)):
        @pl.when(lag >= pieces[number][0])
        def _():
            lag_copy(number).wait_send()
    if peers:
        arrived = sums.at[pl.ds(0, peers)]
        pltpu.make_async_copy(arrived, arrived, sum_recv).wait()
        pltpu.make_async_copy(arrived, arrived, sum_send).wait()
    cells = step_count * n_lag * half * n_sketch * n_probe
    mean = jnp.sum(sums[...], axis=0, keepdims=True) / cells
    factor[...] = jnp.broadcast_to(lax.rsqrt(mean + 1e-06), factor.shape)


def scale_kernel(raw, factor, out, held, sem):
    step_count, probes, columns = raw.shape
    pieces = 2
    part = probes // pieces
    copies = []
    gain = factor[0:1, :]
    for row in range(step_count):
        for piece in range(pieces):
            place = pl.ds(piece * part, part)
            held[row, place] = (raw[row, place] * gain).astype(held.dtype)
            copy = pltpu.make_async_copy(
                held.at[row, place], out.at[row, place], sem.at[row * pieces + piece]
            )
            copy.start()
            copies.append(copy)
    for copy in copies:
        copy.wait()


def scale(raw, factor):
    step_count, probes, columns = raw.shape
    return pl.pallas_call(
        scale_kernel,
        out_shape=jax.ShapeDtypeStruct(raw.shape, jnp.bfloat16),
        in_specs=[pl.BlockSpec(memory_space=pltpu.VMEM)] * 2,
        out_specs=pl.BlockSpec(memory_space=pltpu.HBM),
        scratch_shapes=[
            pltpu.VMEM(raw.shape, jnp.bfloat16),
            pltpu.SemaphoreType.DMA((step_count * 2,)),
        ],
        compiler_params=pltpu.CompilerParams(vmem_limit_bytes=16 * 1024 * 1024),
    )(raw, factor)


def local(sizes, markov, test_matrix):
    n_lag, n_probe, n_sketch = sizes
    step_count, input_count, half = markov.shape
    matrix_rows, _, columns = test_matrix.shape
    lag_total = matrix_rows * n_lag
    steps, pieces = plan(step_count, lag_total)
    count = max(len(pieces), 1)
    pairs = max(n_sketch - 1, 1)
    probes = half * n_sketch
    dma = pltpu.SemaphoreType.DMA
    raw, factor = pl.pallas_call(
        functools.partial(gather_kernel, sizes),
        out_shape=[
            pltpu.VMEM((step_count, probes, columns), jnp.float32),
            pltpu.VMEM((8, columns), jnp.float32),
        ],
        in_specs=[pl.BlockSpec(memory_space=pltpu.HBM)] * 2,
        out_specs=[pl.BlockSpec(memory_space=pltpu.VMEM)] * 2,
        scratch_shapes=[
            pltpu.VMEM((n_sketch, steps, input_count, half), jnp.bfloat16),
            pltpu.VMEM((lag_total, input_count, columns), jnp.bfloat16),
            pltpu.VMEM((steps * input_count, step_count * columns), jnp.bfloat16),
            pltpu.VMEM((n_lag * n_probe, columns), jnp.float32),
            dma, dma, dma, dma,
            dma((pairs,)), dma((pairs,)),
            dma((count,)), dma((count,)),
            dma((count, pairs)), dma((count, pairs)),
            dma, dma,
        ],
        compiler_params=pltpu.CompilerParams(
            collective_id=0, has_side_effects=True, vmem_limit_bytes=59 * 1024 * 1024
        ),
    )(markov, test_matrix)
    return scale(raw, factor)


def solution(mesh):
    sizes = tuple(mesh.shape[name] for name in ("lag", "probe", "sketch"))
    return jax.shard_map(
        functools.partial(local, sizes),
        mesh=mesh,
        in_specs=(P("lag", None, ("probe", "sketch")), P("lag", None, "sketch")),
        out_specs=P("lag", "probe", "sketch"),
        check_vma=False,
    )
```

profile of v0, /device:TPU:0, one launch (start us, length us, event | category | flops | bytes accessed | tf_op | source)
XLA Modules:
  0.0 18.3 jit_solution(10292827557980026421)
XLA Ops:
  0.0 16.9 %shard_map.28 = (f32[4,2048,128]{2,1,0:T(8,128)S(1)}, f32[8,128]{1,0:T(8,128)S(1)}) custom-call(bf16[4,32,1024]{2,1,0:T(8,128)(2,1)} %markov.1, bf16[1,32,128]{2,1,0:T(8,128)(2,1)} %matrix.1), custom_call_target="tpu_custom_call" | custom-call | tf_op jit(solution)/shard_map/pallas_call | solution.py:284
  16.9 1.4 %shard_map.29 = bf16[4,2048,128]{2,1,0:T(8,128)(2,1)} custom-call(f32[4,2048,128]{2,1,0:T(8,128)S(1)} %get-tuple-element.7.raw, f32[8,128]{1,0:T(8,128)S(1)} %get-tuple-element.8.factor), custom_call_target="tpu_custom_call" | custom-call | tf_op jit(solution)/shard_map/pallas_call | solution.py:261
where the time goes:
time: 18.4 us; the launch traced here: 18.3 us
  Pallas kernels  18.3 us (99%)
    pallas_call x1, Pallas kernels, local(): pl.pallas_call(functools.partial(gather_kernel, sizes), out_shape=[pltpu....  16.9 us
    pallas_call x1, Pallas kernels, scale(): pl.pallas_call(scale_kernel, out_shape=jax.ShapeDtypeStruct(raw.shape, jn...  1.41 us

commit v1 on v0

--- a/solution.py
+++ b/solution.py
@@ -237,6 +237,293 @@
     factor[...] = jnp.broadcast_to(lax.rsqrt(mean + 1e-06), factor.shape)
 
 
+def near_kernel(
+    sizes, cut, markov, matrix, raw, factor,
+    window, held, weights, gram, other, sums,
+    own_sem, matrix_own_sem, matrix_send, matrix_recv, pair_send, pair_recv,
+    down_send, down_recv, up_send, up_recv, pass_send, pass_recv, sum_send, sum_recv, all_in,
+):
+    n_lag, n_probe, n_sketch = sizes
+    step_count, input_count, half = markov.shape
+    columns = matrix.shape[2]
+    matrix_rows = matrix.shape[0]
+    lag_total = matrix_rows * n_lag
+    depth = lag_total * input_count
+    later = lag_total - 1
+    alone = step_count - later
+    lag = lax.axis_index("lag")
+    probe = lax.axis_index("probe")
+    sketch = lax.axis_index("sketch")
+    twin = 1 - sketch
+    place = (lag * n_probe + probe) * n_sketch + sketch
+    devices = n_lag * n_probe * n_sketch
+    line = n_lag * n_sketch
+    is_first = lag == 0
+    is_last = lag == n_lag - 1
+    is_head = place == devices - 1
+    below = {"lag": lax.max(lag - 1, 0), "probe": probe, "sketch": sketch}
+    above = {"lag": lax.min(lag + 1, n_lag - 1), "probe": probe, "sketch": sketch}
+    partner = {"lag": lag, "probe": probe, "sketch": twin}
+
+    def device(index):
+        group = lax.div(index, n_sketch)
+        return {
+            "lag": lax.div(group, n_probe),
+            "probe": lax.rem(group, n_probe),
+            "sketch": lax.rem(index, n_sketch),
+        }
+
+    def on_line(index):
+        at = lax.rem(lag * n_sketch + sketch + 1 + index, line)
+        return {"lag": lax.div(at, n_sketch), "probe": probe, "sketch": lax.rem(at, n_sketch)}
+
+    barrier = pltpu.get_barrier_semaphore()
+    loop(line - 1, lambda index: pl.semaphore_signal(
+        barrier, inc=1, device_id=on_line(index), device_id_type=MESH
+    ))
+
+    @pl.when(probe < n_probe - 1)
+    def _():
+        pl.semaphore_signal(barrier, inc=1, device_id=device(devices - 1), device_id_type=MESH)
+
+    own_slots = pl.ds(later, step_count)
+    next_slots = pl.ds(later + step_count, later)
+    own_rows = held.at[sketch, pl.ds(lag * matrix_rows, matrix_rows)]
+    matrix_own = pltpu.make_async_copy(matrix, own_rows, matrix_own_sem)
+    matrix_own.start()
+    own = pltpu.make_async_copy(markov, window.at[sketch, own_slots], own_sem)
+    own.start()
+    weights[...] = jnp.zeros_like(weights)
+
+    @pl.when(is_last)
+    def _():
+        window[:, next_slots] = jnp.zeros((n_sketch, later, input_count, half), window.dtype)
+
+    parts = (pl.ds(0, cut), pl.ds(cut, half - cut))
+
+    def remote(src, dst, send, recv, to):
+        return pltpu.make_async_remote_copy(
+            src_ref=src, dst_ref=dst, send_sem=send, recv_sem=recv, device_id=to, device_id_type=MESH
+        )
+
+    def down(part):
+        return remote(
+            window.at[sketch, pl.ds(later, later), :, parts[part]],
+            window.at[sketch, next_slots, :, parts[part]],
+            down_send.at[part], down_recv.at[part], below,
+        )
+
+    def up():
+        return remote(
+            window.at[sketch, pl.ds(later + alone, later), :, parts[1]],
+            window.at[sketch, pl.ds(0, later), :, parts[1]],
+            up_send, up_recv, above,
+        )
+
+    def passed(part):
+        ref = window.at[sketch, next_slots, :, parts[part]]
+        return remote(ref, ref, pass_send.at[part], pass_recv.at[part], partner)
+
+    pair = remote(
+        window.at[sketch, own_slots], window.at[sketch, own_slots], pair_send, pair_recv, partner
+    )
+
+    matrix_own.wait()
+    pl.semaphore_wait(barrier, lax.select(is_head, devices - 1, line - 1))
+    loop(line - 1, lambda index: remote(own_rows, own_rows, matrix_send, matrix_recv, on_line(index)).start())
+    own.wait()
+
+    @pl.when(jnp.logical_not(is_first))
+    def _():
+        down(0).start()
+
+    @pl.when(jnp.logical_not(is_last))
+    def _():
+        up().start()
+
+    pair.start()
+
+    @pl.when(jnp.logical_not(is_first))
+    def _():
+        down(1).start()
+
+    @pl.when(is_head)
+    def _():
+        loop(devices - 1, lambda index: pl.semaphore_signal(
+            all_in, inc=1, device_id=device(index), device_id_type=MESH
+        ))
+
+    def outer(first, second, start, stop):
+        def rows(slots):
+            slot, count = slots
+            return window[sketch, pl.ds(slot, count), :, start:stop].reshape(count * input_count, stop - start)
+        return lax.dot_general(
+            rows(first), rows(second), (((1,), (1,)), ((), ())), preferred_element_type=jnp.float32
+        )
+
+    inner = outer((later, step_count), (later, step_count), 0, half)
+    gram[...] = jnp.zeros_like(gram)
+
+    def shift(row):
+        low, high = max(0, -row), min(lag_total, step_count - row)
+        to = slice(low * input_count, high * input_count)
+        at = slice((row + low) * input_count, (row + high) * input_count)
+        gram[to, to] += inner[at, at]
+
+    for row in range(step_count):
+        shift(row)
+
+    @pl.when(jnp.logical_not(is_first))
+    def _():
+        for row in range(-later, 0):
+            shift(row)
+
+    def cross(edge):
+        for row in range(alone, step_count):
+            count = (step_count - row) * input_count
+            gram[0:count, count:depth] += 2.0 * edge[(row - alone) * input_count:, 0:(row - alone + 1) * input_count]
+
+    @pl.when(jnp.logical_not(is_first))
+    def _():
+        up().wait_recv()
+        cross(outer((0, later), (later, later), cut, half))
+
+    @pl.when(jnp.logical_not(is_last))
+    def _():
+        down(0).wait_recv()
+        passed(0).start()
+        cross(outer((later + alone, later), (later + step_count, later), 0, cut))
+
+    whole = gram[...]
+    high = whole.astype(jnp.bfloat16)
+    rest = whole - high.astype(jnp.float32)
+    middle = rest.astype(jnp.bfloat16)
+    low = (rest - middle.astype(jnp.float32)).astype(jnp.bfloat16)
+
+    flat = held.reshape(n_sketch * lag_total, input_count, columns)
+    arrived = flat.at[pl.ds(0, n_sketch * lag_total - matrix_rows)]
+    pltpu.make_async_copy(arrived, arrived, matrix_recv).wait()
+    mine = held[sketch].reshape(depth, columns)
+    both = jnp.concatenate([mine, held[twin].reshape(depth, columns)], axis=1)
+    product = jnp.dot(low, both, preferred_element_type=jnp.float32)
+    product = product + jnp.dot(middle, both, preferred_element_type=jnp.float32)
+    product = product + jnp.dot(high, both, preferred_element_type=jnp.float32)
+    square = jnp.sum(product * both.astype(jnp.float32), axis=0, keepdims=True)
+    sums[pl.ds(place, 1), :] = square[:, :columns]
+    other[...] = square[:, columns:]
+
+    def sum_copy(index, side):
+        at = lax.rem(lag * n_probe + probe + index, n_lag * n_probe)
+        to = {"lag": lax.div(at, n_probe), "probe": lax.rem(at, n_probe), "sketch": side}
+        ref = sums.at[pl.ds(place, 1)]
+        src = other if side is twin else ref
+        return remote(src, ref, sum_send, sum_recv, to)
+
+    @pl.when(jnp.logical_not(is_head))
+    def _():
+        pl.semaphore_wait(all_in, 1)
+
+    loop(n_lag * n_probe - 1, lambda index: sum_copy(index + 1, sketch).start())
+    loop(n_lag * n_probe, lambda index: sum_copy(index, twin).start())
+
+    for row in range(step_count):
+        weights[pl.ds(row * input_count, depth), row * columns:(row + 1) * columns] = mine
+
+    tile = 256
+
+    def multiply(side, first, last):
+        for start in range(first, last, tile):
+            block = window[side, pl.ds(later, step_count + later), :, pl.ds(start, tile)]
+            product = lax.dot_general(
+                block.reshape((step_count + later) * input_count, tile), weights[...], (((0,), (0,)), ((), ())),
+                preferred_element_type=jnp.float32,
+            )
+            for row in range(step_count):
+                raw[row, pl.ds(pl.multiple_of(side * half + start, tile), tile), :] = (
+                    product[:, row * columns:(row + 1) * columns]
+                )
+
+    multiply(sketch, 0, cut)
+    pair.wait()
+
+    @pl.when(jnp.logical_not(is_last))
+    def _():
+        passed(0).wait_recv()
+
+    multiply(twin, 0, cut)
+
+    @pl.when(jnp.logical_not(is_last))
+    def _():
+        down(1).wait_recv()
+        passed(1).start()
+
+    multiply(sketch, cut, half)
+
+    @pl.when(jnp.logical_not(is_last))
+    def _():
+        passed(1).wait_recv()
+
+    multiply(twin, cut, half)
+
+    @pl.when(jnp.logical_not(is_last))
+    def _():
+        passed(0).wait_send()
+        passed(1).wait_send()
+        up().wait_send()
+
+    @pl.when(jnp.logical_not(is_first))
+    def _():
+        down(0).wait_send()
+        down(1).wait_send()
+
+    pltpu.make_async_copy(arrived, arrived, matrix_send).wait()
+    landed = sums.at[pl.ds(0, devices - 1)]
+    pltpu.make_async_copy(landed, landed, sum_send).wait()
+    pltpu.make_async_copy(landed, landed, sum_recv).wait()
+    cells = step_count * n_lag * half * n_sketch * n_probe
+    mean = lax.max(jnp.sum(sums[...], axis=0, keepdims=True), 0.0) / cells
+    factor[...] = jnp.broadcast_to(lax.rsqrt(mean + 1e-06), factor.shape)
+
+
+def near(sizes, markov, test_matrix):
+    n_lag, n_probe, n_sketch = sizes
+    step_count, input_count, half = markov.shape
+    matrix_rows, _, columns = test_matrix.shape
+    lag_total = matrix_rows * n_lag
+    later = lag_total - 1
+    dma = pltpu.SemaphoreType.DMA
+    return pl.pallas_call(
+        functools.partial(near_kernel, sizes, half * 3 // 4),
+        out_shape=[
+            pltpu.VMEM((step_count, half * n_sketch, columns), jnp.float32),
+            pltpu.VMEM((8, columns), jnp.float32),
+        ],
+        in_specs=[pl.BlockSpec(memory_space=pltpu.HBM)] * 2,
+        out_specs=[pl.BlockSpec(memory_space=pltpu.VMEM)] * 2,
+        scratch_shapes=[
+            pltpu.VMEM((n_sketch, step_count + 2 * later, input_count, half), jnp.bfloat16),
+            pltpu.VMEM((n_sketch, lag_total, input_count, columns), jnp.bfloat16),
+            pltpu.VMEM(((step_count + later) * input_count, step_count * columns), jnp.bfloat16),
+            pltpu.VMEM((lag_total * input_count, lag_total * input_count), jnp.float32),
+            pltpu.VMEM((1, columns), jnp.float32),
+            pltpu.VMEM((n_lag * n_probe * n_sketch, columns), jnp.float32),
+            dma, dma, dma, dma, dma, dma,
+            dma((2,)), dma((2,)), dma, dma, dma((2,)), dma((2,)), dma, dma,
+            pltpu.SemaphoreType.REGULAR,
+        ],
+        compiler_params=pltpu.CompilerParams(
+            collective_id=1, has_side_effects=True, vmem_limit_bytes=59 * 1024 * 1024
+        ),
+    )(markov, test_matrix)
+
+
+def is_near(sizes, markov, test_matrix):
+    n_lag, n_probe, n_sketch = sizes
+    step_count, input_count, half = markov.shape
+    lag_total = test_matrix.shape[0] * n_lag
+    return n_sketch == 2 and n_lag > 1 and 1 < lag_total <= step_count and half % 512 == 0
+
+
 def scale_kernel(raw, factor, out, held, sem):
     step_count, probes, columns = raw.shape
     pieces = 2
@@ -272,6 +559,8 @@
 
 
 def local(sizes, markov, test_matrix):
+    if is_near(sizes, markov, test_matrix):
+        return scale(*near(sizes, markov, test_matrix))
     n_lag, n_probe, n_sketch = sizes
     step_count, input_count, half = markov.shape
     matrix_rows, _, columns = test_matrix.shape

time: 18.4 us -> 17.8 us (0.967)
  Pallas kernels: 18.3 us -> 17.6 us
    pallas_call x1, Pallas kernels: 16.9 us -> 16.2 us  [near(): pl.pallas_call(functools.partial(near_kernel, sizes, half * 3 // 4), out_...]
where the time goes in v1:
time: 17.8 us; the launch traced here: 17.6 us
  Pallas kernels  17.6 us (99%)
    pallas_call x1, Pallas kernels, near(): pl.pallas_call(functools.partial(near_kernel, sizes, half * 3 // 4), out_...  16.2 us
    pallas_call x1, Pallas kernels, scale(): pl.pallas_call(scale_kernel, out_shape=jax.ShapeDtypeStruct(raw.shape, jn...  1.41 us

profile of v1, /device:TPU:0, one launch (start us, length us, event | category | flops | bytes accessed | tf_op | source)
XLA Modules:
  0.0 17.6 jit_solution(13607452895121865225)
XLA Ops:
  0.0 16.2 %shard_map.28 = (f32[4,2048,128]{2,1,0:T(8,128)S(1)}, f32[8,128]{1,0:T(8,128)S(1)}) custom-call(bf16[4,32,1024]{2,1,0:T(8,128)(2,1)} %markov.1, bf16[1,32,128]{2,1,0:T(8,128)(2,1)} %matrix.1), custom_call_target="tpu_custom_call" | custom-call | tf_op jit(solution)/shard_map/pallas_call | solution.py:495
  16.2 1.4 %shard_map.29 = bf16[4,2048,128]{2,1,0:T(8,128)(2,1)} custom-call(f32[4,2048,128]{2,1,0:T(8,128)S(1)} %get-tuple-element.7.raw, f32[8,128]{1,0:T(8,128)S(1)} %get-tuple-element.8.factor), custom_call_target="tpu_custom_call" | custom-call | tf_op jit(solution)/shard_map/pallas_call | solution.py:548

commit v2 on v1

--- a/solution.py
+++ b/solution.py
@@ -240,7 +240,7 @@
 def near_kernel(
     sizes, cut, markov, matrix, raw, factor,
     window, held, weights, gram, other, sums,
-    own_sem, matrix_own_sem, matrix_send, matrix_recv, pair_send, pair_recv,
+    own_sem, matrix_own_sem, matrix_send, matrix_recv, hand_send, pair_send, pair_recv,
     down_send, down_recv, up_send, up_recv, pass_send, pass_recv, sum_send, sum_recv, all_in,
 ):
     n_lag, n_probe, n_sketch = sizes
@@ -330,7 +330,33 @@
 
     matrix_own.wait()
     pl.semaphore_wait(barrier, lax.select(is_head, devices - 1, line - 1))
-    loop(line - 1, lambda index: remote(own_rows, own_rows, matrix_send, matrix_recv, on_line(index)).start())
+
+    def rows_of(index):
+        return held.at[sketch, pl.ds(index * matrix_rows, matrix_rows)]
+
+    def matrix_copy(to_lag, side):
+        return remote(
+            own_rows, own_rows, matrix_send.at[side, to_lag], matrix_recv.at[side, lag],
+            {"lag": to_lag, "probe": probe, "sketch": sketch if side == 0 else twin},
+        )
+
+    def matrix_hand(index):
+        return remote(
+            rows_of(index), rows_of(index), hand_send.at[index], matrix_recv.at[1, index], partner
+        )
+
+    def matrix_landed(index, side):
+        ref = held.at[sketch if side == 0 else twin, pl.ds(index * matrix_rows, matrix_rows)]
+        pltpu.make_async_copy(ref, ref, matrix_recv.at[side, index]).wait()
+
+    for to_lag in reversed(range(n_lag)):
+        @pl.when(lag != to_lag)
+        def _():
+            matrix_copy(to_lag, 0).start()
+            if to_lag == n_lag - 1:
+                matrix_copy(to_lag, 1).start()
+    own_hand = remote(own_rows, own_rows, matrix_send.at[1, 0], matrix_recv.at[1, lag], partner)
+    own_hand.start()
     own.wait()
 
     @pl.when(jnp.logical_not(is_first))
@@ -383,6 +409,17 @@
             count = (step_count - row) * input_count
             gram[0:count, count:depth] += 2.0 * edge[(row - alone) * input_count:, 0:(row - alone + 1) * input_count]
 
+    def gather_matrix():
+        for index in reversed(range(n_lag)):
+            @pl.when(lag != index)
+            def _():
+                matrix_landed(index, 0)
+                matrix_hand(index).start()
+
+    @pl.when(jnp.logical_not(is_last))
+    def _():
+        gather_matrix()
+
     @pl.when(jnp.logical_not(is_first))
     def _():
         up().wait_recv()
@@ -400,9 +437,12 @@
     middle = rest.astype(jnp.bfloat16)
     low = (rest - middle.astype(jnp.float32)).astype(jnp.bfloat16)
 
-    flat = held.reshape(n_sketch * lag_total, input_count, columns)
-    arrived = flat.at[pl.ds(0, n_sketch * lag_total - matrix_rows)]
-    pltpu.make_async_copy(arrived, arrived, matrix_recv).wait()
+    @pl.when(is_last)
+    def _():
+        for index in range(n_lag - 1):
+            matrix_landed(index, 0)
+    for index in range(n_lag):
+        matrix_landed(index, 1)
     mine = held[sketch].reshape(depth, columns)
     both = jnp.concatenate([mine, held[twin].reshape(depth, columns)], axis=1)
     product = jnp.dot(low, both, preferred_element_type=jnp.float32)
@@ -476,7 +516,17 @@
         down(0).wait_send()
         down(1).wait_send()
 
-    pltpu.make_async_copy(arrived, arrived, matrix_send).wait()
+    own_hand.wait_send()
+    for index in range(n_lag):
+        @pl.when(lag != index)
+        def _():
+            matrix_copy(index, 0).wait_send()
+            if index == n_lag - 1:
+                matrix_copy(index, 1).wait_send()
+
+            @pl.when(jnp.logical_not(is_last))
+            def _():
+                matrix_hand(index).wait_send()
     landed = sums.at[pl.ds(0, devices - 1)]
     pltpu.make_async_copy(landed, landed, sum_send).wait()
     pltpu.make_async_copy(landed, landed, sum_recv).wait()
@@ -507,7 +557,7 @@
             pltpu.VMEM((lag_total * input_count, lag_total * input_count), jnp.float32),
             pltpu.VMEM((1, columns), jnp.float32),
             pltpu.VMEM((n_lag * n_probe * n_sketch, columns), jnp.float32),
-            dma, dma, dma, dma, dma, dma,
+            dma, dma, dma((2, n_lag)), dma((2, n_lag)), dma((n_lag,)), dma, dma,
             dma((2,)), dma((2,)), dma, dma, dma((2,)), dma((2,)), dma, dma,
             pltpu.SemaphoreType.REGULAR,
         ],

time: 17.8 us -> 17.3 us (0.972)
  Pallas kernels: 17.6 us -> 17.1 us
    pallas_call x1, Pallas kernels: 16.2 us -> 15.7 us  [near(): pl.pallas_call(functools.partial(near_kernel, sizes, half * 3 // 4), out_...]
where the time goes in v2:
time: 17.3 us; the launch traced here: 17.1 us
  Pallas kernels  17.1 us (99%)
    pallas_call x1, Pallas kernels, near(): pl.pallas_call(functools.partial(near_kernel, sizes, half * 3 // 4), out_...  15.7 us
    pallas_call x1, Pallas kernels, scale(): pl.pallas_call(scale_kernel, out_shape=jax.ShapeDtypeStruct(raw.shape, jn...  1.41 us

profile of v2, /device:TPU:0, one launch (start us, length us, event | category | flops | bytes accessed | tf_op | source)
XLA Modules:
  0.0 17.1 jit_solution(9721129432965850709)
XLA Ops:
  0.0 15.7 %shard_map.28 = (f32[4,2048,128]{2,1,0:T(8,128)S(1)}, f32[8,128]{1,0:T(8,128)S(1)}) custom-call(bf16[4,32,1024]{2,1,0:T(8,128)(2,1)} %markov.1, bf16[1,32,128]{2,1,0:T(8,128)(2,1)} %matrix.1), custom_call_target="tpu_custom_call" | custom-call | tf_op jit(solution)/shard_map/pallas_call | solution.py:545
  15.7 1.4 %shard_map.29 = bf16[4,2048,128]{2,1,0:T(8,128)(2,1)} custom-call(f32[4,2048,128]{2,1,0:T(8,128)S(1)} %get-tuple-element.7.raw, f32[8,128]{1,0:T(8,128)S(1)} %get-tuple-element.8.factor), custom_call_target="tpu_custom_call" | custom-call | tf_op jit(solution)/shard_map/pallas_call | solution.py:598

commit v3 on v1

--- a/solution.py
+++ b/solution.py
@@ -240,7 +240,7 @@
 def near_kernel(
     sizes, cut, markov, matrix, raw, factor,
     window, held, weights, gram, other, sums,
-    own_sem, matrix_own_sem, matrix_send, matrix_recv, pair_send, pair_recv,
+    own_sem, matrix_own_sem, matrix_send, matrix_recv, twin_send, twin_recv, hand_send, pair_send, pair_recv,
     down_send, down_recv, up_send, up_recv, pass_send, pass_recv, sum_send, sum_recv, all_in,
 ):
     n_lag, n_probe, n_sketch = sizes
@@ -310,7 +310,7 @@
         return remote(
             window.at[sketch, pl.ds(later, later), :, parts[part]],
             window.at[sketch, next_slots, :, parts[part]],
-            down_send.at[part], down_recv.at[part], below,
+            down_send, down_recv.at[part], below,
         )
 
     def up():
@@ -322,7 +322,7 @@
 
     def passed(part):
         ref = window.at[sketch, next_slots, :, parts[part]]
-        return remote(ref, ref, pass_send.at[part], pass_recv.at[part], partner)
+        return remote(ref, ref, pass_send, pass_recv.at[part], partner)
 
     pair = remote(
         window.at[sketch, own_slots], window.at[sketch, own_slots], pair_send, pair_recv, partner
@@ -330,7 +330,21 @@
 
     matrix_own.wait()
     pl.semaphore_wait(barrier, lax.select(is_head, devices - 1, line - 1))
-    loop(line - 1, lambda index: remote(own_rows, own_rows, matrix_send, matrix_recv, on_line(index)).start())
+
+    def matrix_copy(to_lag):
+        to = {"lag": to_lag, "probe": probe, "sketch": sketch}
+        return remote(own_rows, own_rows, matrix_send, matrix_recv, to)
+
+    matrix_twin = remote(
+        own_rows, own_rows, twin_send, twin_recv, {"lag": n_lag - 1, "probe": probe, "sketch": twin}
+    )
+    matrix_hand = remote(held.at[sketch], held.at[sketch], hand_send, twin_recv, partner)
+    for to_lag in reversed(range(n_lag)):
+        @pl.when(lag != to_lag)
+        def _():
+            matrix_copy(to_lag).start()
+        if to_lag == n_lag - 1:
+            matrix_twin.start()
     own.wait()
 
     @pl.when(jnp.logical_not(is_first))
@@ -340,12 +354,6 @@
     @pl.when(jnp.logical_not(is_last))
     def _():
         up().start()
-
-    pair.start()
-
-    @pl.when(jnp.logical_not(is_first))
-    def _():
-        down(1).start()
 
     @pl.when(is_head)
     def _():
@@ -383,6 +391,13 @@
             count = (step_count - row) * input_count
             gram[0:count, count:depth] += 2.0 * edge[(row - alone) * input_count:, 0:(row - alone + 1) * input_count]
 
+    others = held.at[sketch, pl.ds(0, lag_total - matrix_rows)]
+
+    @pl.when(jnp.logical_not(is_last))
+    def _():
+        pltpu.make_async_copy(others, others, matrix_recv).wait()
+        matrix_hand.start()
+
     @pl.when(jnp.logical_not(is_first))
     def _():
         up().wait_recv()
@@ -391,7 +406,6 @@
     @pl.when(jnp.logical_not(is_last))
     def _():
         down(0).wait_recv()
-        passed(0).start()
         cross(outer((later + alone, later), (later + step_count, later), 0, cut))
 
     whole = gram[...]
@@ -400,9 +414,11 @@
     middle = rest.astype(jnp.bfloat16)
     low = (rest - middle.astype(jnp.float32)).astype(jnp.bfloat16)
 
-    flat = held.reshape(n_sketch * lag_total, input_count, columns)
-    arrived = flat.at[pl.ds(0, n_sketch * lag_total - matrix_rows)]
-    pltpu.make_async_copy(arrived, arrived, matrix_recv).wait()
+    @pl.when(is_last)
+    def _():
+        pltpu.make_async_copy(others, others, matrix_recv).wait()
+
+    matrix_hand.wait_recv()
     mine = held[sketch].reshape(depth, columns)
     both = jnp.concatenate([mine, held[twin].reshape(depth, columns)], axis=1)
     product = jnp.dot(low, both, preferred_element_type=jnp.float32)
@@ -425,6 +441,16 @@
 
     loop(n_lag * n_probe - 1, lambda index: sum_copy(index + 1, sketch).start())
     loop(n_lag * n_probe, lambda index: sum_copy(index, twin).start())
+
+    pair.start()
+
+    @pl.when(jnp.logical_not(is_first))
+    def _():
+        down(1).start()
+
+    @pl.when(jnp.logical_not(is_last))
+    def _():
+        passed(0).start()
 
     for row in range(step_count):
         weights[pl.ds(row * input_count, depth), row * columns:(row + 1) * columns] = mine
@@ -465,18 +491,20 @@
 
     multiply(twin, cut, half)
 
-    @pl.when(jnp.logical_not(is_last))
-    def _():
-        passed(0).wait_send()
-        passed(1).wait_send()
+    received = window.at[sketch, next_slots]
+
+    @pl.when(jnp.logical_not(is_last))
+    def _():
+        pltpu.make_async_copy(received, received, pass_send).wait()
+        matrix_hand.wait_send()
         up().wait_send()
 
     @pl.when(jnp.logical_not(is_first))
     def _():
-        down(0).wait_send()
-        down(1).wait_send()
-
-    pltpu.make_async_copy(arrived, arrived, matrix_send).wait()
+        pltpu.make_async_copy(received, received, down_send).wait()
+
+    pltpu.make_async_copy(others, others, matrix_send).wait()
+    matrix_twin.wait_send()
     landed = sums.at[pl.ds(0, devices - 1)]
     pltpu.make_async_copy(landed, landed, sum_send).wait()
     pltpu.make_async_copy(landed, landed, sum_recv).wait()
@@ -507,8 +535,8 @@
             pltpu.VMEM((lag_total * input_count, lag_total * input_count), jnp.float32),
             pltpu.VMEM((1, columns), jnp.float32),
             pltpu.VMEM((n_lag * n_probe * n_sketch, columns), jnp.float32),
-            dma, dma, dma, dma, dma, dma,
-            dma((2,)), dma((2,)), dma, dma, dma((2,)), dma((2,)), dma, dma,
+            dma, dma, dma, dma, dma, dma, dma, dma, dma,
+            dma, dma((2,)), dma, dma, dma, dma((2,)), dma, dma,
             pltpu.SemaphoreType.REGULAR,
         ],
         compiler_params=pltpu.CompilerParams(
@@ -528,19 +556,13 @@
     step_count, probes, columns = raw.shape
     pieces = 2
     part = probes // pieces
-    copies = []
     gain = factor[0:1, :]
     for row in range(step_count):
         for piece in range(pieces):
             place = pl.ds(piece * part, part)
             held[row, place] = (raw[row, place] * gain).astype(held.dtype)
-            copy = pltpu.make_async_copy(
-                held.at[row, place], out.at[row, place], sem.at[row * pieces + piece]
-            )
-            copy.start()
-            copies.append(copy)
-    for copy in copies:
-        copy.wait()
+            pltpu.make_async_copy(held.at[row, place], out.at[row, place], sem).start()
+    pltpu.make_async_copy(held, out, sem).wait()
 
 
 def scale(raw, factor):
@@ -552,7 +574,7 @@
         out_specs=pl.BlockSpec(memory_space=pltpu.HBM),
         scratch_shapes=[
             pltpu.VMEM(raw.shape, jnp.bfloat16),
-            pltpu.SemaphoreType.DMA((step_count * 2,)),
+            pltpu.SemaphoreType.DMA,
         ],
         compiler_params=pltpu.CompilerParams(vmem_limit_bytes=16 * 1024 * 1024),
     )(raw, factor)

time: 17.8 us -> 16.8 us (0.944)
  Pallas kernels: 17.6 us -> 16.6 us
    pallas_call x1, Pallas kernels: 16.2 us -> 15.2 us  [near(): pl.pallas_call(functools.partial(near_kernel, sizes, half * 3 // 4), out_...]
where the time goes in v3:
time: 16.8 us; the launch traced here: 16.6 us
  Pallas kernels  16.6 us (99%)
    pallas_call x1, Pallas kernels, near(): pl.pallas_call(functools.partial(near_kernel, sizes, half * 3 // 4), out_...  15.2 us
    pallas_call x1, Pallas kernels, scale(): pl.pallas_call(scale_kernel, out_shape=jax.ShapeDtypeStruct(raw.shape, jn...  1.34 us

profile of v3, /device:TPU:0, one launch (start us, length us, event | category | flops | bytes accessed | tf_op | source)
XLA Modules:
  0.0 16.6 jit_solution(13046845399264545015)
XLA Ops:
  0.0 15.2 %shard_map.28 = (f32[4,2048,128]{2,1,0:T(8,128)S(1)}, f32[8,128]{1,0:T(8,128)S(1)}) custom-call(bf16[4,32,1024]{2,1,0:T(8,128)(2,1)} %markov.1, bf16[1,32,128]{2,1,0:T(8,128)(2,1)} %matrix.1), custom_call_target="tpu_custom_call" | custom-call | tf_op jit(solution)/shard_map/pallas_call | solution.py:523
  15.3 1.3 %shard_map.29 = bf16[4,2048,128]{2,1,0:T(8,128)(2,1)} custom-call(f32[4,2048,128]{2,1,0:T(8,128)S(1)} %get-tuple-element.7.raw, f32[8,128]{1,0:T(8,128)S(1)} %get-tuple-element.8.factor), custom_call_target="tpu_custom_call" | custom-call | tf_op jit(solution)/shard_map/pallas_call | solution.py:570

commit v4 on v3

--- a/solution.py
+++ b/solution.py
@@ -241,7 +241,7 @@
     sizes, cut, markov, matrix, raw, factor,
     window, held, weights, gram, other, sums,
     own_sem, matrix_own_sem, matrix_send, matrix_recv, twin_send, twin_recv, hand_send, pair_send, pair_recv,
-    down_send, down_recv, up_send, up_recv, pass_send, pass_recv, sum_send, sum_recv, all_in,
+    down_send, down_recv, up_send, up_recv, pass_send, pass_recv, sum_send, sum_recv, all_in, risen,
 ):
     n_lag, n_probe, n_sketch = sizes
     step_count, input_count, half = markov.shape
@@ -257,7 +257,6 @@
     twin = 1 - sketch
     place = (lag * n_probe + probe) * n_sketch + sketch
     devices = n_lag * n_probe * n_sketch
-    line = n_lag * n_sketch
     is_first = lag == 0
     is_last = lag == n_lag - 1
     is_head = place == devices - 1
@@ -273,18 +272,40 @@
             "sketch": lax.rem(index, n_sketch),
         }
 
-    def on_line(index):
-        at = lax.rem(lag * n_sketch + sketch + 1 + index, line)
-        return {"lag": lax.div(at, n_sketch), "probe": probe, "sketch": lax.rem(at, n_sketch)}
+    last = n_lag - 1
+
+    def at_lag(to_lag, side):
+        return {"lag": to_lag, "probe": probe, "sketch": side}
 
     barrier = pltpu.get_barrier_semaphore()
-    loop(line - 1, lambda index: pl.semaphore_signal(
-        barrier, inc=1, device_id=on_line(index), device_id_type=MESH
-    ))
+
+    def greet(to):
+        pl.semaphore_signal(barrier, inc=1, device_id=to, device_id_type=MESH)
+
+    @pl.when(jnp.logical_not(is_first))
+    def _():
+        greet(at_lag(0, sketch))
+
+    @pl.when(is_last)
+    def _():
+        greet(at_lag(0, twin))
+
+    @pl.when(jnp.logical_not(is_last))
+    def _():
+        greet(at_lag(last, twin))
+
+    for to_lag in range(1, n_lag):
+        @pl.when(lag < to_lag)
+        def _():
+            greet(at_lag(to_lag, sketch))
+
+    greet(partner)
 
     @pl.when(probe < n_probe - 1)
     def _():
-        pl.semaphore_signal(barrier, inc=1, device_id=device(devices - 1), device_id_type=MESH)
+        greet(device(devices - 1))
+
+    expected = lax.select(is_first, n_lag + 1, lax.select(is_last, 2 * n_lag - 1, lag + 1))
 
     own_slots = pl.ds(later, step_count)
     next_slots = pl.ds(later + step_count, later)
@@ -328,39 +349,6 @@
         window.at[sketch, own_slots], window.at[sketch, own_slots], pair_send, pair_recv, partner
     )
 
-    matrix_own.wait()
-    pl.semaphore_wait(barrier, lax.select(is_head, devices - 1, line - 1))
-
-    def matrix_copy(to_lag):
-        to = {"lag": to_lag, "probe": probe, "sketch": sketch}
-        return remote(own_rows, own_rows, matrix_send, matrix_recv, to)
-
-    matrix_twin = remote(
-        own_rows, own_rows, twin_send, twin_recv, {"lag": n_lag - 1, "probe": probe, "sketch": twin}
-    )
-    matrix_hand = remote(held.at[sketch], held.at[sketch], hand_send, twin_recv, partner)
-    for to_lag in reversed(range(n_lag)):
-        @pl.when(lag != to_lag)
-        def _():
-            matrix_copy(to_lag).start()
-        if to_lag == n_lag - 1:
-            matrix_twin.start()
-    own.wait()
-
-    @pl.when(jnp.logical_not(is_first))
-    def _():
-        down(0).start()
-
-    @pl.when(jnp.logical_not(is_last))
-    def _():
-        up().start()
-
-    @pl.when(is_head)
-    def _():
-        loop(devices - 1, lambda index: pl.semaphore_signal(
-            all_in, inc=1, device_id=device(index), device_id_type=MESH
-        ))
-
     def outer(first, second, start, stop):
         def rows(slots):
             slot, count = slots
@@ -369,22 +357,88 @@
             rows(first), rows(second), (((1,), (1,)), ((), ())), preferred_element_type=jnp.float32
         )
 
-    inner = outer((later, step_count), (later, step_count), 0, half)
-    gram[...] = jnp.zeros_like(gram)
-
-    def shift(row):
-        low, high = max(0, -row), min(lag_total, step_count - row)
-        to = slice(low * input_count, high * input_count)
-        at = slice((row + low) * input_count, (row + high) * input_count)
-        gram[to, to] += inner[at, at]
-
-    for row in range(step_count):
-        shift(row)
+    def own_gram():
+        inner = outer((later, step_count), (later, step_count), 0, half)
+        gram[...] = jnp.zeros_like(gram)
+
+        def shift(row):
+            low, high = max(0, -row), min(lag_total, step_count - row)
+            to = slice(low * input_count, high * input_count)
+            at = slice((row + low) * input_count, (row + high) * input_count)
+            gram[to, to] += inner[at, at]
+
+        for row in range(step_count):
+            shift(row)
+
+        @pl.when(jnp.logical_not(is_first))
+        def _():
+            for row in range(-later, 0):
+                shift(row)
+
+    def matrix_copy(to_lag):
+        return remote(own_rows, own_rows, matrix_send, matrix_recv, at_lag(to_lag, sketch))
+
+    matrix_twin = remote(own_rows, own_rows, twin_send, twin_recv, at_lag(last, twin))
+    matrix_hand = remote(held.at[sketch], held.at[sketch], hand_send, twin_recv, partner)
+
+    def rise(to_lag, semaphore, side):
+        pl.semaphore_signal(semaphore, inc=1, device_id=at_lag(to_lag, side), device_id_type=MESH)
+
+    @pl.when(is_first)
+    def _():
+        own.wait()
+        own_gram()
+
+    pl.semaphore_wait(barrier, lax.select(is_head, devices - 1, expected))
+    for from_lag in range(2, n_lag):
+        @pl.when(lag == from_lag)
+        def _():
+            for to_lag in range(1, from_lag):
+                rise(to_lag, risen.at[from_lag], sketch)
+                if from_lag == last:
+                    rise(to_lag, risen.at[0], twin)
+
+    matrix_own.wait()
+
+    @pl.when(is_first)
+    def _():
+        matrix_copy(last).start()
+        matrix_twin.start()
+        for to_lag in reversed(range(1, last)):
+            matrix_copy(to_lag).start()
+        up().start()
 
     @pl.when(jnp.logical_not(is_first))
     def _():
-        for row in range(-later, 0):
-            shift(row)
+        own.wait()
+        for to_lag in range(last):
+            @pl.when(lag > to_lag)
+            def _():
+                matrix_copy(to_lag).start()
+        down(0).start()
+
+        @pl.when(is_last)
+        def _():
+            matrix_twin.start()
+
+        own_gram()
+
+    for here in range(1, last):
+        @pl.when(lag == here)
+        def _():
+            for to_lag in range(here + 1, n_lag):
+                pl.semaphore_wait(risen.at[to_lag], 1)
+                if to_lag == here + 1:
+                    up().start()
+                matrix_copy(to_lag).start()
+            pl.semaphore_wait(risen.at[0], 1)
+            matrix_twin.start()
+
+    @pl.when(is_head)
+    def _():
+        loop(devices - 1, lambda index: pl.semaphore_signal(
+            all_in, inc=1, device_id=device(index), device_id_type=MESH
+        ))
 
     def cross(edge):
         for row in range(alone, step_count):
@@ -397,6 +451,10 @@
     def _():
         pltpu.make_async_copy(others, others, matrix_recv).wait()
         matrix_hand.start()
+
+    @pl.when(jnp.logical_not(jnp.logical_or(is_first, is_last)))
+    def _():
+        down(1).start()
 
     @pl.when(jnp.logical_not(is_first))
     def _():
@@ -442,11 +500,11 @@
     loop(n_lag * n_probe - 1, lambda index: sum_copy(index + 1, sketch).start())
     loop(n_lag * n_probe, lambda index: sum_copy(index, twin).start())
 
+    @pl.when(is_last)
+    def _():
+        down(1).start()
+
     pair.start()
-
-    @pl.when(jnp.logical_not(is_first))
-    def _():
-        down(1).start()
 
     @pl.when(jnp.logical_not(is_last))
     def _():
@@ -455,7 +513,7 @@
     for row in range(step_count):
         weights[pl.ds(row * input_count, depth), row * columns:(row + 1) * columns] = mine
 
-    tile = 256
+    tile = 128
 
     def multiply(side, first, last):
         for start in range(first, last, tile):
@@ -521,7 +579,7 @@
     later = lag_total - 1
     dma = pltpu.SemaphoreType.DMA
     return pl.pallas_call(
-        functools.partial(near_kernel, sizes, half * 3 // 4),
+        functools.partial(near_kernel, sizes, half * 5 // 8),
         out_shape=[
             pltpu.VMEM((step_count, half * n_sketch, columns), jnp.float32),
             pltpu.VMEM((8, columns), jnp.float32),
@@ -538,6 +596,7 @@
             dma, dma, dma, dma, dma, dma, dma, dma, dma,
             dma, dma((2,)), dma, dma, dma, dma((2,)), dma, dma,
             pltpu.SemaphoreType.REGULAR,
+            pltpu.SemaphoreType.REGULAR((n_lag,)),
         ],
         compiler_params=pltpu.CompilerParams(
             collective_id=1, has_side_effects=True, vmem_limit_bytes=59 * 1024 * 1024

time: 16.8 us -> 16.4 us (0.976)
  Pallas kernels: 16.6 us -> 16.2 us
    pallas_call x1, Pallas kernels: 15.2 us -> 14.9 us  [near(): pl.pallas_call(functools.partial(near_kernel, sizes, half * 5 // 8), out_...]
where the time goes in v4:
time: 16.4 us; the launch traced here: 16.3 us
  Pallas kernels  16.2 us (99%)
    pallas_call x1, Pallas kernels, near(): pl.pallas_call(functools.partial(near_kernel, sizes, half * 5 // 8), out_...  14.9 us
    pallas_call x1, Pallas kernels, scale(): pl.pallas_call(scale_kernel, out_shape=jax.ShapeDtypeStruct(raw.shape, jn...  1.34 us

profile of v4, /device:TPU:0, one launch (start us, length us, event | category | flops | bytes accessed | tf_op | source)
XLA Modules:
  0.0 16.3 jit_solution(8437400482018984329)
XLA Ops:
  0.0 14.9 %shard_map.28 = (f32[4,2048,128]{2,1,0:T(8,128)S(1)}, f32[8,128]{1,0:T(8,128)S(1)}) custom-call(bf16[4,32,1024]{2,1,0:T(8,128)(2,1)} %markov.1, bf16[1,32,128]{2,1,0:T(8,128)(2,1)} %matrix.1), custom_call_target="tpu_custom_call" | custom-call | tf_op jit(solution)/shard_map/pallas_call | solution.py:581
  14.9 1.3 %shard_map.29 = bf16[4,2048,128]{2,1,0:T(8,128)(2,1)} custom-call(f32[4,2048,128]{2,1,0:T(8,128)S(1)} %get-tuple-element.7.raw, f32[8,128]{1,0:T(8,128)S(1)} %get-tuple-element.8.factor), custom_call_target="tpu_custom_call" | custom-call | tf_op jit(solution)/shard_map/pallas_call | solution.py:629

commit v5 on v4

--- a/solution.py
+++ b/solution.py
@@ -238,9 +238,9 @@
 
 
 def near_kernel(
-    sizes, cut, markov, matrix, raw, factor,
+    sizes, cuts, markov, matrix, raw, factor,
     window, held, weights, gram, other, sums,
-    own_sem, matrix_own_sem, matrix_send, matrix_recv, twin_send, twin_recv, hand_send, pair_send, pair_recv,
+    own_sem, matrix_own_sem, matrix_send, matrix_recv, first_recv, twin_send, twin_recv, hand_send, pair_send, pair_recv,
     down_send, down_recv, up_send, up_recv, pass_send, pass_recv, sum_send, sum_recv, all_in, risen,
 ):
     n_lag, n_probe, n_sketch = sizes
@@ -259,7 +259,9 @@
     devices = n_lag * n_probe * n_sketch
     is_first = lag == 0
     is_last = lag == n_lag - 1
-    is_head = place == devices - 1
+    is_middle = jnp.logical_not(jnp.logical_or(is_first, is_last))
+    head = n_probe * n_sketch - 1
+    is_head = place == head
     below = {"lag": lax.max(lag - 1, 0), "probe": probe, "sketch": sketch}
     above = {"lag": lax.min(lag + 1, n_lag - 1), "probe": probe, "sketch": sketch}
     partner = {"lag": lag, "probe": probe, "sketch": twin}
@@ -285,14 +287,7 @@
     @pl.when(jnp.logical_not(is_first))
     def _():
         greet(at_lag(0, sketch))
-
-    @pl.when(is_last)
-    def _():
         greet(at_lag(0, twin))
-
-    @pl.when(jnp.logical_not(is_last))
-    def _():
-        greet(at_lag(last, twin))
 
     for to_lag in range(1, n_lag):
         @pl.when(lag < to_lag)
@@ -303,9 +298,9 @@
 
     @pl.when(probe < n_probe - 1)
     def _():
-        greet(device(devices - 1))
-
-    expected = lax.select(is_first, n_lag + 1, lax.select(is_last, 2 * n_lag - 1, lag + 1))
+        greet(device(head))
+
+    expected = lax.select(is_first, 2 * n_lag - 1, lag + 1)
 
     own_slots = pl.ds(later, step_count)
     next_slots = pl.ds(later + step_count, later)
@@ -320,29 +315,38 @@
     def _():
         window[:, next_slots] = jnp.zeros((n_sketch, later, input_count, half), window.dtype)
 
-    parts = (pl.ds(0, cut), pl.ds(cut, half - cut))
+    def parts(edge):
+        return pl.ds(0, cuts[edge]), pl.ds(cuts[edge], half - cuts[edge])
 
     def remote(src, dst, send, recv, to):
         return pltpu.make_async_remote_copy(
             src_ref=src, dst_ref=dst, send_sem=send, recv_sem=recv, device_id=to, device_id_type=MESH
         )
 
-    def down(part):
+    def down(part, edge):
         return remote(
-            window.at[sketch, pl.ds(later, later), :, parts[part]],
-            window.at[sketch, next_slots, :, parts[part]],
+            window.at[sketch, pl.ds(later, later), :, parts(edge)[part]],
+            window.at[sketch, next_slots, :, parts(edge)[part]],
             down_send, down_recv.at[part], below,
         )
 
-    def up():
+    def up(edge):
         return remote(
-            window.at[sketch, pl.ds(later + alone, later), :, parts[1]],
-            window.at[sketch, pl.ds(0, later), :, parts[1]],
+            window.at[sketch, pl.ds(later + alone, later), :, parts(edge)[1]],
+            window.at[sketch, pl.ds(0, later), :, parts(edge)[1]],
             up_send, up_recv, above,
         )
 
-    def passed(part):
-        ref = window.at[sketch, next_slots, :, parts[part]]
+    def edge_above(body):
+        for edge in range(2):
+            pl.when(is_first if edge == 0 else is_middle)(functools.partial(body, edge))
+
+    def edge_below(body):
+        for edge in range(2):
+            pl.when(lag == 1 if edge == 0 else lag > 1)(functools.partial(body, edge))
+
+    def passed(part, edge):
+        ref = window.at[sketch, next_slots, :, parts(edge)[part]]
         return remote(ref, ref, pass_send, pass_recv.at[part], partner)
 
     pair = remote(
@@ -375,14 +379,15 @@
             for row in range(-later, 0):
                 shift(row)
 
-    def matrix_copy(to_lag):
-        return remote(own_rows, own_rows, matrix_send, matrix_recv, at_lag(to_lag, sketch))
-
-    matrix_twin = remote(own_rows, own_rows, twin_send, twin_recv, at_lag(last, twin))
+    def matrix_copy(to_lag, recv=matrix_recv):
+        return remote(own_rows, own_rows, matrix_send, recv, at_lag(to_lag, sketch))
+
+    def matrix_twin(to_lag):
+        return remote(own_rows, own_rows, twin_send, twin_recv, at_lag(to_lag, twin))
+
     matrix_hand = remote(held.at[sketch], held.at[sketch], hand_send, twin_recv, partner)
-
-    def rise(to_lag, semaphore, side):
-        pl.semaphore_signal(semaphore, inc=1, device_id=at_lag(to_lag, side), device_id_type=MESH)
+    rest_rows = held.at[sketch, pl.ds(matrix_rows, lag_total - matrix_rows)]
+    rest_hand = remote(rest_rows, rest_rows, hand_send, twin_recv, partner)
 
     @pl.when(is_first)
     def _():
@@ -394,19 +399,18 @@
         @pl.when(lag == from_lag)
         def _():
             for to_lag in range(1, from_lag):
-                rise(to_lag, risen.at[from_lag], sketch)
-                if from_lag == last:
-                    rise(to_lag, risen.at[0], twin)
+                pl.semaphore_signal(
+                    risen.at[from_lag], inc=1, device_id=at_lag(to_lag, sketch), device_id_type=MESH
+                )
 
     matrix_own.wait()
 
     @pl.when(is_first)
     def _():
-        matrix_copy(last).start()
-        matrix_twin.start()
-        for to_lag in reversed(range(1, last)):
-            matrix_copy(to_lag).start()
-        up().start()
+        for to_lag in reversed(range(1, n_lag)):
+            matrix_copy(to_lag, first_recv).start()
+            matrix_twin(to_lag).start()
+        up(0).start()
 
     @pl.when(jnp.logical_not(is_first))
     def _():
@@ -415,11 +419,11 @@
             @pl.when(lag > to_lag)
             def _():
                 matrix_copy(to_lag).start()
-        down(0).start()
+        edge_below(lambda edge: down(0, edge).start())
 
         @pl.when(is_last)
         def _():
-            matrix_twin.start()
+            matrix_twin(last).start()
 
         own_gram()
 
@@ -429,15 +433,14 @@
             for to_lag in range(here + 1, n_lag):
                 pl.semaphore_wait(risen.at[to_lag], 1)
                 if to_lag == here + 1:
-                    up().start()
+                    up(1).start()
                 matrix_copy(to_lag).start()
-            pl.semaphore_wait(risen.at[0], 1)
-            matrix_twin.start()
+            matrix_twin(last).start()
 
     @pl.when(is_head)
     def _():
         loop(devices - 1, lambda index: pl.semaphore_signal(
-            all_in, inc=1, device_id=device(index), device_id_type=MESH
+            all_in, inc=1, device_id=device(lax.rem(place + 1 + index, devices)), device_id_type=MESH
         ))
 
     def cross(edge):
@@ -447,24 +450,32 @@
 
     others = held.at[sketch, pl.ds(0, lag_total - matrix_rows)]
 
-    @pl.when(jnp.logical_not(is_last))
+    middle_rows = held.at[sketch, pl.ds(0, lag_total - 2 * matrix_rows)]
+
+    @pl.when(is_first)
     def _():
         pltpu.make_async_copy(others, others, matrix_recv).wait()
         matrix_hand.start()
 
-    @pl.when(jnp.logical_not(jnp.logical_or(is_first, is_last)))
-    def _():
-        down(1).start()
-
-    @pl.when(jnp.logical_not(is_first))
-    def _():
-        up().wait_recv()
-        cross(outer((0, later), (later, later), cut, half))
-
-    @pl.when(jnp.logical_not(is_last))
-    def _():
-        down(0).wait_recv()
-        cross(outer((later + alone, later), (later + step_count, later), 0, cut))
+    @pl.when(is_middle)
+    def _():
+        pltpu.make_async_copy(middle_rows, middle_rows, matrix_recv).wait()
+        rest_hand.start()
+
+    @pl.when(is_middle)
+    def _():
+        edge_below(lambda edge: down(1, edge).start())
+
+    def from_below(edge):
+        up(edge).wait_recv()
+        cross(outer((0, later), (later, later), cuts[edge], half))
+
+    def from_above(edge):
+        down(0, edge).wait_recv()
+        cross(outer((later + alone, later), (later + step_count, later), 0, cuts[edge]))
+
+    edge_below(from_below)
+    edge_above(from_above)
 
     whole = gram[...]
     high = whole.astype(jnp.bfloat16)
@@ -474,7 +485,12 @@
 
     @pl.when(is_last)
     def _():
-        pltpu.make_async_copy(others, others, matrix_recv).wait()
+        if n_lag > 2:
+            pltpu.make_async_copy(middle_rows, middle_rows, matrix_recv).wait()
+
+    @pl.when(jnp.logical_not(is_first))
+    def _():
+        pltpu.make_async_copy(own_rows, own_rows, first_recv).wait()
 
     matrix_hand.wait_recv()
     mine = held[sketch].reshape(depth, columns)
@@ -502,13 +518,11 @@
 
     @pl.when(is_last)
     def _():
-        down(1).start()
+        down(1, 1).start()
 
     pair.start()
 
-    @pl.when(jnp.logical_not(is_last))
-    def _():
-        passed(0).start()
+    edge_above(lambda edge: passed(0, edge).start())
 
     for row in range(step_count):
         weights[pl.ds(row * input_count, depth), row * columns:(row + 1) * columns] = mine
@@ -527,42 +541,51 @@
                     product[:, row * columns:(row + 1) * columns]
                 )
 
+    cut = min(cuts)
     multiply(sketch, 0, cut)
     pair.wait()
 
+    edge_above(lambda edge: passed(0, edge).wait_recv())
+
+    multiply(twin, 0, cut)
+
+    def hand_rest(edge):
+        down(1, edge).wait_recv()
+        passed(1, edge).start()
+
+    edge_above(hand_rest)
+
+    multiply(sketch, cut, half)
+
+    edge_above(lambda edge: passed(1, edge).wait_recv())
+
+    multiply(twin, cut, half)
+
+    received = window.at[sketch, next_slots]
+
     @pl.when(jnp.logical_not(is_last))
     def _():
-        passed(0).wait_recv()
-
-    multiply(twin, 0, cut)
-
-    @pl.when(jnp.logical_not(is_last))
-    def _():
-        down(1).wait_recv()
-        passed(1).start()
-
-    multiply(sketch, cut, half)
-
-    @pl.when(jnp.logical_not(is_last))
-    def _():
-        passed(1).wait_recv()
-
-    multiply(twin, cut, half)
-
-    received = window.at[sketch, next_slots]
-
-    @pl.when(jnp.logical_not(is_last))
-    def _():
         pltpu.make_async_copy(received, received, pass_send).wait()
+        edge_above(lambda edge: up(edge).wait_send())
+
+    @pl.when(is_first)
+    def _():
         matrix_hand.wait_send()
-        up().wait_send()
+        pltpu.make_async_copy(others, others, twin_send).wait()
 
     @pl.when(jnp.logical_not(is_first))
     def _():
+        matrix_twin(last).wait_send()
+
+        @pl.when(jnp.logical_not(is_last))
+        def _():
+            rest_hand.wait_send()
+
+    @pl.when(jnp.logical_not(is_first))
+    def _():
         pltpu.make_async_copy(received, received, down_send).wait()
 
     pltpu.make_async_copy(others, others, matrix_send).wait()
-    matrix_twin.wait_send()
     landed = sums.at[pl.ds(0, devices - 1)]
     pltpu.make_async_copy(landed, landed, sum_send).wait()
     pltpu.make_async_copy(landed, landed, sum_recv).wait()
@@ -579,7 +602,7 @@
     later = lag_total - 1
     dma = pltpu.SemaphoreType.DMA
     return pl.pallas_call(
-        functools.partial(near_kernel, sizes, half * 5 // 8),
+        functools.partial(near_kernel, sizes, (half * 3 // 4, half * 5 // 8)),
         out_shape=[
             pltpu.VMEM((step_count, half * n_sketch, columns), jnp.float32),
             pltpu.VMEM((8, columns), jnp.float32),
@@ -593,7 +616,7 @@
             pltpu.VMEM((lag_total * input_count, lag_total * input_count), jnp.float32),
             pltpu.VMEM((1, columns), jnp.float32),
             pltpu.VMEM((n_lag * n_probe * n_sketch, columns), jnp.float32),
-            dma, dma, dma, dma, dma, dma, dma, dma, dma,
+            dma, dma, dma, dma, dma, dma, dma, dma, dma, dma,
             dma, dma((2,)), dma, dma, dma, dma((2,)), dma, dma,
             pltpu.SemaphoreType.REGULAR,
             pltpu.SemaphoreType.REGULAR((n_lag,)),
@@ -608,7 +631,7 @@
     n_lag, n_probe, n_sketch = sizes
     step_count, input_count, half = markov.shape
     lag_total = test_matrix.shape[0] * n_lag
-    return n_sketch == 2 and n_lag > 1 and 1 < lag_total <= step_count and half % 512 == 0
+    return n_sketch == 2 and n_lag > 2 and 1 < lag_total <= step_count and half % 512 == 0
 
 
 def scale_kernel(raw, factor, out, held, sem):

time: 16.4 us -> 16.2 us (0.988)
  Pallas kernels: 16.2 us -> 16 us
    pallas_call x1, Pallas kernels: 14.9 us -> 14.7 us  [near(): pl.pallas_call(functools.partial(near_kernel, sizes, (half * 3 // 4, half...]
where the time goes in v5:
time: 16.2 us; the launch traced here: 16 us
  Pallas kernels  16 us (99%)
    pallas_call x1, Pallas kernels, near(): pl.pallas_call(functools.partial(near_kernel, sizes, (half * 3 // 4, half...  14.7 us
    pallas_call x1, Pallas kernels, scale(): pl.pallas_call(scale_kernel, out_shape=jax.ShapeDtypeStruct(raw.shape, jn...  1.34 us

profile of v5, /device:TPU:0, one launch (start us, length us, event | category | flops | bytes accessed | tf_op | source)
XLA Modules:
  0.0 16.0 jit_solution(1344127152872418770)
XLA Ops:
  0.0 14.7 %shard_map.28 = (f32[4,2048,128]{2,1,0:T(8,128)S(1)}, f32[8,128]{1,0:T(8,128)S(1)}) custom-call(bf16[4,32,1024]{2,1,0:T(8,128)(2,1)} %markov.1, bf16[1,32,128]{2,1,0:T(8,128)(2,1)} %matrix.1), custom_call_target="tpu_custom_call" | custom-call | tf_op jit(solution)/shard_map/pallas_call | solution.py:604
  14.7 1.3 %shard_map.29 = bf16[4,2048,128]{2,1,0:T(8,128)(2,1)} custom-call(f32[4,2048,128]{2,1,0:T(8,128)S(1)} %get-tuple-element.7.raw, f32[8,128]{1,0:T(8,128)S(1)} %get-tuple-element.8.factor), custom_call_target="tpu_custom_call" | custom-call | tf_op jit(solution)/shard_map/pallas_call | solution.py:652

commit v6 on v5

--- a/solution.py
+++ b/solution.py
@@ -239,7 +239,7 @@
 
 def near_kernel(
     sizes, cuts, markov, matrix, raw, factor,
-    window, held, weights, gram, other, sums,
+    window, held, weights, gram, joint, other, sums,
     own_sem, matrix_own_sem, matrix_send, matrix_recv, first_recv, twin_send, twin_recv, hand_send, pair_send, pair_recv,
     down_send, down_recv, up_send, up_recv, pass_send, pass_recv, sum_send, sum_recv, all_in, risen,
 ):
@@ -364,6 +364,7 @@
     def own_gram():
         inner = outer((later, step_count), (later, step_count), 0, half)
         gram[...] = jnp.zeros_like(gram)
+        joint[...] = jnp.zeros_like(joint)
 
         def shift(row):
             low, high = max(0, -row), min(lag_total, step_count - row)
@@ -468,14 +469,15 @@
 
     def from_below(edge):
         up(edge).wait_recv()
-        cross(outer((0, later), (later, later), cuts[edge], half))
+        joint[...] += outer((0, later), (later, later), cuts[edge], half)
 
     def from_above(edge):
         down(0, edge).wait_recv()
-        cross(outer((later + alone, later), (later + step_count, later), 0, cuts[edge]))
+        joint[...] += outer((later + alone, later), (later + step_count, later), 0, cuts[edge])
 
     edge_below(from_below)
     edge_above(from_above)
+    cross(joint[...])
 
     whole = gram[...]
     high = whole.astype(jnp.bfloat16)
@@ -502,8 +504,7 @@
     sums[pl.ds(place, 1), :] = square[:, :columns]
     other[...] = square[:, columns:]
 
-    def sum_copy(index, side):
-        at = lax.rem(lag * n_probe + probe + index, n_lag * n_probe)
+    def sum_copy(at, side):
         to = {"lag": lax.div(at, n_probe), "probe": lax.rem(at, n_probe), "sketch": side}
         ref = sums.at[pl.ds(place, 1)]
         src = other if side is twin else ref
@@ -513,8 +514,14 @@
     def _():
         pl.semaphore_wait(all_in, 1)
 
-    loop(n_lag * n_probe - 1, lambda index: sum_copy(index + 1, sketch).start())
-    loop(n_lag * n_probe, lambda index: sum_copy(index, twin).start())
+    group = lag * n_probe + probe
+
+    def send_sums(index):
+        sum_copy(index, twin).start()
+        sum_copy(lax.select(index < group, index, index + 1), sketch).start()
+
+    loop(n_lag * n_probe - 1, send_sums)
+    sum_copy(n_lag * n_probe - 1, twin).start()
 
     @pl.when(is_last)
     def _():
@@ -614,6 +621,7 @@
             pltpu.VMEM((n_sketch, lag_total, input_count, columns), jnp.bfloat16),
             pltpu.VMEM(((step_count + later) * input_count, step_count * columns), jnp.bfloat16),
             pltpu.VMEM((lag_total * input_count, lag_total * input_count), jnp.float32),
+            pltpu.VMEM((later * input_count, later * input_count), jnp.float32),
             pltpu.VMEM((1, columns), jnp.float32),
             pltpu.VMEM((n_lag * n_probe * n_sketch, columns), jnp.float32),
             dma, dma, dma, dma, dma, dma, dma, dma, dma, dma,
@@ -636,7 +644,7 @@
 
 def scale_kernel(raw, factor, out, held, sem):
     step_count, probes, columns = raw.shape
-    pieces = 2
+    pieces = 8
     part = probes // pieces
     gain = factor[0:1, :]
     for row in range(step_count):

time: 16.2 us -> 16.1 us (level)
  no operation moved by 1% of the time
where the time goes in v6:
time: 16.1 us; the launch traced here: 15.9 us
  Pallas kernels  15.9 us (99%)
    pallas_call x1, Pallas kernels, near(): pl.pallas_call(functools.partial(near_kernel, sizes, (half * 3 // 4, half...  14.6 us
    pallas_call x1, Pallas kernels, scale(): pl.pallas_call(scale_kernel, out_shape=jax.ShapeDtypeStruct(raw.shape, jn...  1.3 us

profile of v6, /device:TPU:0, one launch (start us, length us, event | category | flops | bytes accessed | tf_op | source)
XLA Modules:
  0.0 15.9 jit_solution(2671062778791633527)
XLA Ops:
  0.0 14.6 %shard_map.28 = (f32[4,2048,128]{2,1,0:T(8,128)S(1)}, f32[8,128]{1,0:T(8,128)S(1)}) custom-call(bf16[4,32,1024]{2,1,0:T(8,128)(2,1)} %markov.1, bf16[1,32,128]{2,1,0:T(8,128)(2,1)} %matrix.1), custom_call_target="tpu_custom_call" | custom-call | tf_op jit(solution)/shard_map/pallas_call | solution.py:611
  14.6 1.3 %shard_map.29 = bf16[4,2048,128]{2,1,0:T(8,128)(2,1)} custom-call(f32[4,2048,128]{2,1,0:T(8,128)S(1)} %get-tuple-element.7.raw, f32[8,128]{1,0:T(8,128)S(1)} %get-tuple-element.8.factor), custom_call_target="tpu_custom_call" | custom-call | tf_op jit(solution)/shard_map/pallas_call | solution.py:660

commit v7 on v6

--- a/solution.py
+++ b/solution.py
@@ -241,7 +241,7 @@
     sizes, cuts, markov, matrix, raw, factor,
     window, held, weights, gram, joint, other, sums,
     own_sem, matrix_own_sem, matrix_send, matrix_recv, first_recv, twin_send, twin_recv, hand_send, pair_send, pair_recv,
-    down_send, down_recv, up_send, up_recv, pass_send, pass_recv, sum_send, sum_recv, all_in, risen,
+    down_send, down_recv, up_send, up_recv, pass_recv, sum_send, sum_recv, all_in, risen,
 ):
     n_lag, n_probe, n_sketch = sizes
     step_count, input_count, half = markov.shape
@@ -347,7 +347,7 @@
 
     def passed(part, edge):
         ref = window.at[sketch, next_slots, :, parts(edge)[part]]
-        return remote(ref, ref, pass_send, pass_recv.at[part], partner)
+        return remote(ref, ref, pair_send, pass_recv.at[part], partner)
 
     pair = remote(
         window.at[sketch, own_slots], window.at[sketch, own_slots], pair_send, pair_recv, partner
@@ -401,7 +401,7 @@
         def _():
             for to_lag in range(1, from_lag):
                 pl.semaphore_signal(
-                    risen.at[from_lag], inc=1, device_id=at_lag(to_lag, sketch), device_id_type=MESH
+                    risen.at[from_lag - 2], inc=1, device_id=at_lag(to_lag, sketch), device_id_type=MESH
                 )
 
     matrix_own.wait()
@@ -415,11 +415,11 @@
 
     @pl.when(jnp.logical_not(is_first))
     def _():
-        own.wait()
         for to_lag in range(last):
             @pl.when(lag > to_lag)
             def _():
                 matrix_copy(to_lag).start()
+        own.wait()
         edge_below(lambda edge: down(0, edge).start())
 
         @pl.when(is_last)
@@ -432,7 +432,7 @@
         @pl.when(lag == here)
         def _():
             for to_lag in range(here + 1, n_lag):
-                pl.semaphore_wait(risen.at[to_lag], 1)
+                pl.semaphore_wait(risen.at[to_lag - 2], 1)
                 if to_lag == here + 1:
                     up(1).start()
                 matrix_copy(to_lag).start()
@@ -550,7 +550,7 @@
 
     cut = min(cuts)
     multiply(sketch, 0, cut)
-    pair.wait()
+    pair.wait_recv()
 
     edge_above(lambda edge: passed(0, edge).wait_recv())
 
@@ -570,9 +570,14 @@
 
     received = window.at[sketch, next_slots]
 
+    @pl.when(is_last)
+    def _():
+        pair.wait_send()
+
     @pl.when(jnp.logical_not(is_last))
     def _():
-        pltpu.make_async_copy(received, received, pass_send).wait()
+        sent = window.at[sketch, pl.ds(later, step_count + later)]
+        pltpu.make_async_copy(sent, sent, pair_send).wait()
         edge_above(lambda edge: up(edge).wait_send())
 
     @pl.when(is_first)
@@ -609,7 +614,7 @@
     later = lag_total - 1
     dma = pltpu.SemaphoreType.DMA
     return pl.pallas_call(
-        functools.partial(near_kernel, sizes, (half * 3 // 4, half * 5 // 8)),
+        functools.partial(near_kernel, sizes, (half * 7 // 8, half * 5 // 8)),
         out_shape=[
             pltpu.VMEM((step_count, half * n_sketch, columns), jnp.float32),
             pltpu.VMEM((8, columns), jnp.float32),
@@ -625,9 +630,9 @@
             pltpu.VMEM((1, columns), jnp.float32),
             pltpu.VMEM((n_lag * n_probe * n_sketch, columns), jnp.float32),
             dma, dma, dma, dma, dma, dma, dma, dma, dma, dma,
-            dma, dma((2,)), dma, dma, dma, dma((2,)), dma, dma,
+            dma, dma((2,)), dma, dma, dma((2,)), dma, dma,
             pltpu.SemaphoreType.REGULAR,
-            pltpu.SemaphoreType.REGULAR((n_lag,)),
+            pltpu.SemaphoreType.REGULAR((n_lag - 2,)),
         ],
         compiler_params=pltpu.CompilerParams(
             collective_id=1, has_side_effects=True, vmem_limit_bytes=59 * 1024 * 1024

time: 16.1 us -> 15.9 us (0.988)
  Pallas kernels: 15.9 us -> 15.7 us
    pallas_call x1, Pallas kernels: 14.6 us -> 14.4 us  [near(): pl.pallas_call(functools.partial(near_kernel, sizes, (half * 7 // 8, half...]
where the time goes in v7:
time: 15.9 us; the launch traced here: 15.7 us
  Pallas kernels  15.7 us (99%)
    pallas_call x1, Pallas kernels, near(): pl.pallas_call(functools.partial(near_kernel, sizes, (half * 7 // 8, half...  14.4 us
    pallas_call x1, Pallas kernels, scale(): pl.pallas_call(scale_kernel, out_shape=jax.ShapeDtypeStruct(raw.shape, jn...  1.3 us

profile of v7, /device:TPU:0, one launch (start us, length us, event | category | flops | bytes accessed | tf_op | source)
XLA Modules:
  0.0 15.7 jit_solution(13883033465670243962)
XLA Ops:
  0.0 14.4 %shard_map.28 = (f32[4,2048,128]{2,1,0:T(8,128)S(1)}, f32[8,128]{1,0:T(8,128)S(1)}) custom-call(bf16[4,32,1024]{2,1,0:T(8,128)(2,1)} %markov.1, bf16[1,32,128]{2,1,0:T(8,128)(2,1)} %matrix.1), custom_call_target="tpu_custom_call" | custom-call | tf_op jit(solution)/shard_map/pallas_call | solution.py:616
  14.4 1.3 %shard_map.29 = bf16[4,2048,128]{2,1,0:T(8,128)(2,1)} custom-call(f32[4,2048,128]{2,1,0:T(8,128)S(1)} %get-tuple-element.7.raw, f32[8,128]{1,0:T(8,128)S(1)} %get-tuple-element.8.factor), custom_call_target="tpu_custom_call" | custom-call | tf_op jit(solution)/shard_map/pallas_call | solution.py:665

commit v8 on v7

--- a/solution.py
+++ b/solution.py
@@ -467,6 +467,8 @@
     def _():
         edge_below(lambda edge: down(1, edge).start())
 
+    pair.start()
+
     def from_below(edge):
         up(edge).wait_recv()
         joint[...] += outer((0, later), (later, later), cuts[edge], half)
@@ -497,9 +499,10 @@
     matrix_hand.wait_recv()
     mine = held[sketch].reshape(depth, columns)
     both = jnp.concatenate([mine, held[twin].reshape(depth, columns)], axis=1)
-    product = jnp.dot(low, both, preferred_element_type=jnp.float32)
-    product = product + jnp.dot(middle, both, preferred_element_type=jnp.float32)
-    product = product + jnp.dot(high, both, preferred_element_type=jnp.float32)
+    product = jnp.dot(
+        jnp.concatenate([low, middle, high], axis=1), jnp.concatenate([both, both, both], axis=0),
+        preferred_element_type=jnp.float32,
+    )
     square = jnp.sum(product * both.astype(jnp.float32), axis=0, keepdims=True)
     sums[pl.ds(place, 1), :] = square[:, :columns]
     other[...] = square[:, columns:]
@@ -526,8 +529,6 @@
     @pl.when(is_last)
     def _():
         down(1, 1).start()
-
-    pair.start()
 
     edge_above(lambda edge: passed(0, edge).start())
 
@@ -649,7 +650,7 @@
 
 def scale_kernel(raw, factor, out, held, sem):
     step_count, probes, columns = raw.shape
-    pieces = 8
+    pieces = 16
     part = probes // pieces
     gain = factor[0:1, :]
     for row in range(step_count):

time: 15.9 us -> 15.8 us (level)
  no operation moved by 1% of the time
where the time goes in v8:
time: 15.8 us; the launch traced here: 15.7 us
  Pallas kernels  15.7 us (99%)
    pallas_call x1, Pallas kernels, near(): pl.pallas_call(functools.partial(near_kernel, sizes, (half * 7 // 8, half...  14.4 us
    pallas_call x1, Pallas kernels, scale(): pl.pallas_call(scale_kernel, out_shape=jax.ShapeDtypeStruct(raw.shape, jn...  1.29 us

profile of v8, /device:TPU:0, one launch (start us, length us, event | category | flops | bytes accessed | tf_op | source)
XLA Modules:
  0.0 15.7 jit_solution(6203715487931722395)
XLA Ops:
  0.0 14.4 %shard_map.28 = (f32[4,2048,128]{2,1,0:T(8,128)S(1)}, f32[8,128]{1,0:T(8,128)S(1)}) custom-call(bf16[4,32,1024]{2,1,0:T(8,128)(2,1)} %markov.1, bf16[1,32,128]{2,1,0:T(8,128)(2,1)} %matrix.1), custom_call_target="tpu_custom_call" | custom-call | tf_op jit(solution)/shard_map/pallas_call | solution.py:617
  14.4 1.3 %shard_map.29 = bf16[4,2048,128]{2,1,0:T(8,128)(2,1)} custom-call(f32[4,2048,128]{2,1,0:T(8,128)S(1)} %get-tuple-element.7.raw, f32[8,128]{1,0:T(8,128)S(1)} %get-tuple-element.8.factor), custom_call_target="tpu_custom_call" | custom-call | tf_op jit(solution)/shard_map/pallas_call | solution.py:666
